TPU v7x, 512 devices: a whole 4x4x16 slice. The times are simulated.
512 devices in a mesh: segment: 4 (over x), cells: 128 (over z, y, core).
Axes of the slice: x: 4, y: 4, z: 16, core: 2. Of those that a mesh axis runs over, the one named last changes fastest.
Arguments:
- feats: bfloat16 [1, 32768, 256], P(None, 'cells'), may hold values from -6 to 6
- weights: bfloat16 [4, 256, 256], P('segment'), may hold values from -0.375 to 0.375
- gains: float32 [4, 256], P('segment'), may hold values from 0.25 to 1.75
- send_rows: int32 [1, 128, 128, 2], P(None, 'cells'), may hold values from 0 to 255, as said below
- send_count: int32 [1, 128, 128], P(None, 'cells'), may hold values from 1 to 2, as said below
- local_index: int32 [1, 128, 4, 2], P(None, 'cells'), may hold values from 0 to 1, as said below
- halo_index: int32 [1, 128, 2, 2], P(None, 'cells'), may hold values from 0 to 3, as said below
- block_count: int32 [1, 128, 2], P(None, 'cells'), may hold values from 1 to 4, as said below
- local_vals: bfloat16 [1, 512, 128, 128], P(None, 'cells'), may hold values from -0.3125 to 0.3125
- halo_vals: bfloat16 [1, 256, 128, 128], P(None, 'cells'), may hold values from -0.3125 to 0.3125
- cotangent: bfloat16 [1, 32768, 256], P(None, 'cells'), may hold values from -6 to 6
Outputs:
- layer_outputs: bfloat16 [4, 1, 32768, 256], P('segment', None, 'cells')
- input_grads: bfloat16 [4, 1, 32768, 256], P('segment', None, 'cells')
- weight_grads: float32 [4, 256, 256], P('segment')
- gain_grads: float32 [4, 256], P('segment')
Inputs may be any that keep to these rules, and one draw needn't show every extreme that they name: `send_rows`: local row indices of the sender. `send_count`: in every slab, every sender fills all slots to some owner, and some owner is filled by every sender. `local_index`: row blocks and column blocks of the owner's own cells. `halo_index`: row blocks of own cells, and column blocks 2 and on for received rows. `block_count`: column 0 counts own blocks, at most 4; column 1 counts received blocks, at most 2; in every slab for each kind some owner has every block of that kind live.
All inputs are finite; a program needn't handle non-finite values.
Results may differ from a plain program's by a relative error of at most 0.015.
Values may be sent and summed in bfloat16 or wider, within the bound.
A program may use at most 64 MiB of HBM per device.

v0:
```python
import math

import jax
import jax.numpy as jnp
from jax import lax
from jax.sharding import PartitionSpec as P

EPS = 1e-05
COEF = 0.7978845608028654


def passed_along(value, axis, steps):
    count = lax.axis_size(axis)
    initial, last = (max(0, -steps), min(count, count - steps))
    return lax.ppermute(value, axis, [(source, source + steps) for source in range(initial, last)])


def gelu_pair(inputs):
    inner = jnp.tanh(COEF * (inputs + 0.044715 * inputs * inputs * inputs))
    value = 0.5 * inputs * (1.0 + inner)
    slope = 0.5 * (1.0 + inner) + 0.5 * inputs * (1.0 - inner * inner) * COEF * (
        1.0 + 3.0 * 0.044715 * inputs * inputs
    )
    return (value, slope)


def block_product(source, index_list, values, live_count, offset, out_blocks):
    block_size = values.shape[-1]
    feat_width = source.shape[-1]
    listed = index_list.shape[0]
    live_mask = (jnp.arange(listed) < live_count).astype(values.dtype)
    masked = values * live_mask[:, None, None]
    picked_tiles = source.reshape(-1, block_size, feat_width)[index_list[:, 1] - offset]
    product = jnp.einsum("bij,bjd->bid", masked, picked_tiles, preferred_element_type=jnp.float32)
    select = (index_list[:, 0][None, :] == jnp.arange(out_blocks)[:, None]).astype(jnp.float32)
    summed = jnp.einsum("rb,bid->rid", select, product, precision=lax.Precision.HIGHEST)
    return summed.reshape(out_blocks * block_size, feat_width)


def block_transpose(grad_rows, index_list, values, live_count, offset, out_blocks):
    block_size = values.shape[-1]
    feat_width = grad_rows.shape[-1]
    listed = index_list.shape[0]
    live_mask = (jnp.arange(listed) < live_count).astype(values.dtype)
    masked = values * live_mask[:, None, None]
    picked_tiles = grad_rows.reshape(-1, block_size, feat_width)[index_list[:, 0]]
    product = jnp.einsum("bij,bid->bjd", masked, picked_tiles, preferred_element_type=jnp.float32)
    select = ((index_list[:, 1] - offset)[None, :] == jnp.arange(out_blocks)[:, None]).astype(
        jnp.float32
    )
    summed = jnp.einsum("cb,bjd->cjd", select, product, precision=lax.Precision.HIGHEST)
    return summed.reshape(out_blocks * block_size, feat_width)


def pick(array, index):
    return lax.dynamic_index_in_dim(array, index, 0, keepdims=False)


def place(array, index, value, valid):
    older = pick(array, index)
    return lax.dynamic_update_index_in_dim(array, jnp.where(valid, value, older), index, 0)


def on_device(
    feats,
    weights,
    gains,
    send_rows,
    send_count,
    local_index,
    halo_index,
    block_count,
    local_vals,
    halo_vals,
    cotangent,
):
    segment_count = lax.axis_size("segment")
    segment_here = lax.axis_index("segment")
    cell_count = lax.axis_size("cells")
    micro_count, rows_dev, feat_width = feats.shape
    block_size = local_vals.shape[-1]
    row_blocks = rows_dev // block_size
    slot_count = send_rows.shape[-1]
    halo_blocks = cell_count * slot_count // block_size
    weight = weights[0]
    gain_row = gains[0]
    ticks = micro_count + segment_count - 1
    scale = 1.0 / math.sqrt(micro_count * cell_count * rows_dev)

    def graph_of(index):
        targets = pick(send_rows, index)[0].reshape(-1)
        live_slot = (jnp.arange(slot_count)[None, :] < pick(send_count, index)[0][:, None]).reshape(
            -1, 1
        )
        counts = pick(block_count, index)[0]
        return (
            targets,
            live_slot,
            pick(local_index, index)[0],
            pick(halo_index, index)[0],
            counts[0],
            counts[1],
            pick(local_vals, index),
            pick(halo_vals, index),
        )

    def activate(summed):
        inverse = lax.rsqrt(jnp.mean(summed * summed, axis=-1, keepdims=True) + EPS)
        normed = summed * inverse * gain_row
        value, slope = gelu_pair(normed)
        return (inverse, value.astype(jnp.bfloat16), slope)

    incoming = jnp.zeros((rows_dev, feat_width), jnp.bfloat16)
    saved_sums = jnp.zeros((micro_count, rows_dev, feat_width), jnp.float32)
    layer_out = jnp.zeros_like(feats)
    for tick in range(ticks):
        offset = tick - segment_here
        valid = (offset >= 0) & (offset < micro_count)
        index = jnp.clip(offset, 0, micro_count - 1)
        current = jnp.where(segment_here == 0, pick(feats, index), incoming)
        graph = graph_of(index)
        picked = current[graph[0]]
        received = lax.all_to_all(
            jnp.where(graph[1], picked, jnp.zeros_like(picked)),
            "cells",
            split_axis=0,
            concat_axis=0,
            tiled=True,
        )
        (
            aggregate_targets,
            aggregate_live_slot,
            aggregate_local_list,
            aggregate_halo_list,
            aggregate_local_live,
            aggregate_halo_live,
            aggregate_own_tiles,
            aggregate_far_tiles,
        ) = graph
        extended = jnp.concatenate([current, received], axis=0)
        summed = block_product(
            extended, aggregate_local_list, aggregate_own_tiles, aggregate_local_live, 0, row_blocks
        ) + block_product(
            extended, aggregate_halo_list, aggregate_far_tiles, aggregate_halo_live, 0, row_blocks
        )
        inverse, activated, slope = activate(summed)
        branch = jnp.dot(activated, weight, preferred_element_type=jnp.float32)
        result = (current.astype(jnp.float32) + branch).astype(jnp.bfloat16)
        saved_sums = place(saved_sums, index, summed, valid)
        layer_out = place(layer_out, index, result, valid)
        if tick + 1 < ticks:
            incoming = passed_along(result, "segment", 1)
    incoming_grad = jnp.zeros((rows_dev, feat_width), jnp.bfloat16)
    grad_weight = jnp.zeros((feat_width, feat_width), jnp.float32)
    grad_gain = jnp.zeros((feat_width,), jnp.float32)
    input_grad = jnp.zeros_like(feats)
    for tick in range(ticks):
        offset = tick - (segment_count - 1 - segment_here)
        valid = (offset >= 0) & (offset < micro_count)
        index = jnp.clip(offset, 0, micro_count - 1)
        graph = graph_of(index)
        targets, live_slot, local_list, halo_list, local_live, halo_live, own_tiles, far_tiles = (
            graph
        )
        upstream = jnp.where(
            segment_here == segment_count - 1, pick(cotangent, index), incoming_grad
        )
        summed = pick(saved_sums, index)
        inverse, activated, slope = activate(summed)
        term_weight = jnp.dot(activated.T, upstream, preferred_element_type=jnp.float32)
        grad_act = jnp.dot(upstream, weight.T, preferred_element_type=jnp.float32)
        grad_normed = grad_act * slope
        term_gain = jnp.sum(grad_normed * summed * inverse, axis=0)
        grad_scaled = grad_normed * gain_row
        grad_summed = (
            inverse
            * (
                grad_scaled
                - summed
                * inverse
                * inverse
                * jnp.mean(grad_scaled * summed, axis=-1, keepdims=True)
            )
        ).astype(jnp.bfloat16)
        own_part = block_transpose(grad_summed, local_list, own_tiles, local_live, 0, row_blocks)
        far_part = block_transpose(
            grad_summed, halo_list, far_tiles, halo_live, row_blocks, halo_blocks
        ).astype(jnp.bfloat16)
        returned = lax.all_to_all(far_part, "cells", split_axis=0, concat_axis=0, tiled=True)
        returned = jnp.where(live_slot, returned, jnp.zeros_like(returned)).astype(jnp.float32)
        spread = jnp.zeros((rows_dev, feat_width), jnp.float32).at[targets].add(returned)
        result = (upstream.astype(jnp.float32) + own_part + spread).astype(jnp.bfloat16)
        grad_weight = grad_weight + jnp.where(valid, term_weight, jnp.zeros_like(term_weight))
        grad_gain = grad_gain + jnp.where(valid, term_gain, jnp.zeros_like(term_gain))
        input_grad = place(input_grad, index, result, valid)
        if tick + 1 < ticks:
            incoming_grad = passed_along(result, "segment", -1)
    grad_weight, grad_gain = lax.psum((grad_weight, grad_gain), "cells")
    return (
        layer_out[None],
        input_grad[None],
        (grad_weight * scale)[None],
        (grad_gain * scale)[None],
    )


def solution(mesh):
    in_specs = (
        P(None, "cells", None),
        P("segment", None, None),
        P("segment", None),
        P(None, "cells", None, None),
        P(None, "cells", None),
        P(None, "cells", None, None),
        P(None, "cells", None, None),
        P(None, "cells", None),
        P(None, "cells", None, None),
        P(None, "cells", None, None),
        P(None, "cells", None),
    )
    out_specs = (
        P("segment", None, "cells", None),
        P("segment", None, "cells", None),
        P("segment", None, None),
        P("segment", None),
    )
    return jax.shard_map(
        on_device, mesh=mesh, in_specs=in_specs, out_specs=out_specs, check_vma=False
    )
```

profile of v0, /device:TPU:1, one launch (start us, length us, event | category | flops | bytes accessed | tf_op | source)
XLA Modules:
  0.0 627.6 jit_solution(709606484992422616)
XLA Ops:
  7.2 0.8 iota_compare_fusion
  8.0 0.8 copy.79
  9.0 1.2 gather_fusion
  10.2 0.9 broadcast_select_fusion.3
  11.1 20.7 %all-to-all-start = ((bf16[128,2,256]{2,1,0:T(2,128)(2,1)}), bf16[128,2,256]{2,1,0:T(2,128)(2,1)S(1)}, u32[]{:S(2)}, u32[]{:S(2)}) async-start(bf16[128,2,256]{2,1,0:T(2,128)(2,1)} %broadcast_select_fusion.3), calls=%async_computation | async-start | bytes 262144 | tf_op jit(solution)/shard_map/all_to_all | solution.py:123
  35.3 12.5 %all-to-all-done = bf16[128,2,256]{2,1,0:T(2,128)(2,1)S(1)} async-done(((bf16[128,2,256]{2,1,0:T(2,128)(2,1)}), bf16[128,2,256]{2,1,0:T(2,128)(2,1)S(1)}, u32[]{:S(2)}, u32[]{:S(2)}) %all-to-all-start) | async-done | bytes 131104 | tf_op jit(solution)/shard_map/all_to_all | solution.py:123
  49.6 0.7 fusion.80
  50.8 0.9 fusion.18
  51.8 0.7 copy-done.5
  52.9 3.1 collective-permute-start
  56.0 2.5 collective-permute-done
  58.5 1.2 gather_fusion.3
  59.9 24.1 %all_to_all.72 = bf16[128,2,256]{2,1,0:T(2,128)(2,1)S(1)} all-to-all(bf16[128,2,256]{2,1,0:T(2,128)(2,1)S(1)} %broadcast_select_fusion.2), channel_id=1, replica_groups=mesh['segment'=4,'cells'=128] {'cells'}, dimensions={0} | all-to-all | bytes 262144 | tf_op jit(solution)/shard_map/all_to_all | solution.py:123
  85.5 0.7 fusion.78
  86.5 0.9 fusion.16
  87.9 4.6 collective-permute-start.1
  92.5 1.9 collective-permute-done.1
  94.5 1.2 gather_fusion.6
  95.9 23.8 %all_to_all.73 = bf16[128,2,256]{2,1,0:T(2,128)(2,1)S(1)} all-to-all(bf16[128,2,256]{2,1,0:T(2,128)(2,1)S(1)} %broadcast_select_fusion.1), channel_id=1, replica_groups=mesh['segment'=4,'cells'=128] {'cells'}, dimensions={0} | all-to-all | bytes 262144 | tf_op jit(solution)/shard_map/all_to_all | solution.py:123
  121.2 0.7 fusion.76
  122.1 0.9 fusion.14
  123.5 4.1 collective-permute-start.2
  127.7 2.5 collective-permute-done.2
  130.1 1.2 gather_fusion.9
  131.4 0.9 broadcast_select_fusion
  132.3 7.9 %all-to-all-start.3 = ((bf16[128,2,256]{2,1,0:T(2,128)(2,1)}), bf16[128,2,256]{2,1,0:T(2,128)(2,1)S(1)}, u32[]{:S(2)}, u32[]{:S(2)}) async-start(bf16[128,2,256]{2,1,0:T(2,128)(2,1)} %broadcast_select_fusion), calls=%async_computation.3 | async-start | bytes 262144 | tf_op jit(solution)/shard_map/all_to_all | solution.py:123
  140.4 15.6 %all-to-all-done.3 = bf16[128,2,256]{2,1,0:T(2,128)(2,1)S(1)} async-done(((bf16[128,2,256]{2,1,0:T(2,128)(2,1)}), bf16[128,2,256]{2,1,0:T(2,128)(2,1)S(1)}, u32[]{:S(2)}, u32[]{:S(2)}) %all-to-all-start.3) | async-done | bytes 131104 | tf_op jit(solution)/shard_map/all_to_all | solution.py:123
  157.4 0.7 fusion.74
  158.4 0.9 fusion.12
  162.5 0.7 convolution_convert_fusion.3
  163.3 0.7 convert_element_type.215
  164.0 7.3 %all-to-all-start.4 = ((bf16[128,2,256]{2,1,0:T(2,128)(2,1)}), bf16[128,2,256]{2,1,0:T(2,128)(2,1)S(1)}, u32[]{:S(2)}, u32[]{:S(2)}) async-start(bf16[128,2,256]{2,1,0:T(2,128)(2,1)} %convert_element_type.215), calls=%async_computation.4 | async-start | bytes 262144 | tf_op jit(solution)/shard_map/all_to_all | solution.py:189
  171.6 0.9 fusion.10
  172.8 14.6 %all-to-all-done.4 = bf16[128,2,256]{2,1,0:T(2,128)(2,1)S(1)} async-done(((bf16[128,2,256]{2,1,0:T(2,128)(2,1)}), bf16[128,2,256]{2,1,0:T(2,128)(2,1)S(1)}, u32[]{:S(2)}, u32[]{:S(2)}) %all-to-all-start.4) | async-done | bytes 131104 | tf_op jit(solution)/shard_map/all_to_all | solution.py:189
  187.4 2.2 scatter_custom_fusion
  189.6 1.3 collective-permute-start.3
  191.1 6.1 collective-permute-done.3
  199.3 0.7 convolution_convert_fusion.2
  200.0 0.7 convert_element_type.221
  200.7 7.9 %all-to-all-start.5 = ((bf16[128,2,256]{2,1,0:T(2,128)(2,1)}), bf16[128,2,256]{2,1,0:T(2,128)(2,1)S(1)}, u32[]{:S(2)}, u32[]{:S(2)}) async-start(bf16[128,2,256]{2,1,0:T(2,128)(2,1)} %convert_element_type.221), calls=%async_computation.5 | async-start | bytes 262144 | tf_op jit(solution)/shard_map/all_to_all | solution.py:189
  209.0 0.9 fusion.8
  209.9 14.5 %all-to-all-done.5 = bf16[128,2,256]{2,1,0:T(2,128)(2,1)S(1)} async-done(((bf16[128,2,256]{2,1,0:T(2,128)(2,1)}), bf16[128,2,256]{2,1,0:T(2,128)(2,1)S(1)}, u32[]{:S(2)}, u32[]{:S(2)}) %all-to-all-start.5) | async-done | bytes 131104 | tf_op jit(solution)/shard_map/all_to_all | solution.py:189
  224.5 2.2 scatter_custom_fusion.1
  226.7 1.3 collective-permute-start.4
  228.0 0.9 fusion.85
  228.9 4.4 collective-permute-done.4
  235.3 0.7 convolution_convert_fusion.1
  236.0 0.7 convert_element_type.227
  236.7 8.0 %all-to-all-start.6 = ((bf16[128,2,256]{2,1,0:T(2,128)(2,1)}), bf16[128,2,256]{2,1,0:T(2,128)(2,1)S(1)}, u32[]{:S(2)}, u32[]{:S(2)}) async-start(bf16[128,2,256]{2,1,0:T(2,128)(2,1)} %convert_element_type.227), calls=%async_computation.6 | async-start | bytes 262144 | tf_op jit(solution)/shard_map/all_to_all | solution.py:189
  245.1 0.9 fusion.6
  246.0 14.8 %all-to-all-done.6 = bf16[128,2,256]{2,1,0:T(2,128)(2,1)S(1)} async-done(((bf16[128,2,256]{2,1,0:T(2,128)(2,1)}), bf16[128,2,256]{2,1,0:T(2,128)(2,1)S(1)}, u32[]{:S(2)}, u32[]{:S(2)}) %all-to-all-start.6) | async-done | bytes 131104 | tf_op jit(solution)/shard_map/all_to_all | solution.py:189
  260.9 2.2 scatter_custom_fusion.2
  263.1 1.3 collective-permute-start.5
  264.6 5.0 collective-permute-done.5
  271.6 0.7 convolution_convert_fusion
  272.3 0.7 convert_element_type.233
  273.0 7.9 %all-to-all-start.7 = ((bf16[128,2,256]{2,1,0:T(2,128)(2,1)}), bf16[128,2,256]{2,1,0:T(2,128)(2,1)S(1)}, u32[]{:S(2)}, u32[]{:S(2)}) async-start(bf16[128,2,256]{2,1,0:T(2,128)(2,1)} %convert_element_type.233), calls=%async_computation.7 | async-start | bytes 262144 | tf_op jit(solution)/shard_map/all_to_all | solution.py:189
  281.6 0.9 fusion.4
  282.8 0.9 fusion.1
  283.7 247.4 %psum.15 = f32[256]{0:T(256)S(1)} all-reduce(f32[256]{0:T(256)S(1)} %select_add_fusion), channel_id=1, replica_groups=mesh['segment'=4,'cells'=128] {'cells'}, use_global_device_ids=true, to_apply=%region_18.19 | all-reduce | flops 256 | bytes 2048 | tf_op jit(solution)/shard_map/psum | solution.py:198
  531.7 84.0 %all-reduce.2.cloned.1.call-done = f32[256,256]{1,0:T(8,128)} async-done(((f32[256,256]{1,0:T(8,128)}), f32[256,256]{1,0:T(8,128)}) %all-reduce.2.cloned.1.call-update) | async-done | bytes 262160 | tf_op jit(solution)/shard_map/psum | solution.py:198
  615.7 1.7 multiply_bitcast_fusion
  617.4 2.2 scatter_custom_fusion.3
  619.6 0.7 select_bitcast_fusion
  (138 shorter events, 25.8 us)
Async XLA Ops:
  7.2 45.5 %copy-start = (bf16[1,256,256]{2,1,0:T(8,128)(2,1)S(1)}, bf16[1,256,256]{2,1,0:T(8,128)(2,1)}, u32[]{:S(2)}) copy-start(bf16[1,256,256]{2,1,0:T(8,128)(2,1)} %param.12) | copy-start | bytes 393220
  7.2 1.8 copy-start.4
  11.1 20.7 %copy-start.7 = (s32[1,1,2]{2,1,0:T(1,128)S(1)}, s32[1,1,2]{2,1,0:T(1,128)}, u32[]{:S(2)}) copy-start(s32[1,1,2]{2,1,0:T(1,128)} %param.18) | copy-start | bytes 28
  11.1 36.8 %all-to-all-start = ((bf16[128,2,256]{2,1,0:T(2,128)(2,1)}), bf16[128,2,256]{2,1,0:T(2,128)(2,1)S(1)}, u32[]{:S(2)}, u32[]{:S(2)}) async-start(bf16[128,2,256]{2,1,0:T(2,128)(2,1)} %broadcast_select_fusion.3), calls=%async_computation | async-start | bytes 262144 | tf_op jit(solution)/shard_map/all_to_all | solution.py:123
  33.0 0.7 copy-start.6
  34.6 0.7 copy-start.8
  48.5 0.8 copy-start.2
  49.6 0.9 copy-start.1
  51.8 0.7 copy-start.5
  52.9 5.6 collective-permute-start
  87.9 6.6 %collective-permute-start.1 = (bf16[256,256]{1,0:T(8,128)(2,1)S(1)}, bf16[256,256]{1,0:T(8,128)(2,1)S(1)}, u32[]{:S(2)}, u32[]{:S(2)}) collective-permute-start(bf16[256,256]{1,0:T(8,128)(2,1)S(1)} %add_convert_fusion.2), channel_id=1, source_target_pairs={{0,128},{128,256},{256,384},{1,129},{129,257},{257,385},{2,130},{1... | collective-permute-start | bytes 393224 | tf_op jit(solution)/shard_map/ppermute | solution.py:15
  123.5 6.6 %collective-permute-start.2 = (bf16[256,256]{1,0:T(8,128)(2,1)S(1)}, bf16[256,256]{1,0:T(8,128)(2,1)S(1)}, u32[]{:S(2)}, u32[]{:S(2)}) collective-permute-start(bf16[256,256]{1,0:T(8,128)(2,1)S(1)} %add_convert_fusion.1), channel_id=1, source_target_pairs={{0,128},{128,256},{256,384},{1,129},{129,257},{257,385},{2,130},{1... | collective-permute-start | bytes 393224 | tf_op jit(solution)/shard_map/ppermute | solution.py:15
  132.3 23.7 %all-to-all-start.3 = ((bf16[128,2,256]{2,1,0:T(2,128)(2,1)}), bf16[128,2,256]{2,1,0:T(2,128)(2,1)S(1)}, u32[]{:S(2)}, u32[]{:S(2)}) async-start(bf16[128,2,256]{2,1,0:T(2,128)(2,1)} %broadcast_select_fusion), calls=%async_computation.3 | async-start | bytes 262144 | tf_op jit(solution)/shard_map/all_to_all | solution.py:123
  159.7 0.9 copy-start.3
  164.0 23.3 %all-to-all-start.4 = ((bf16[128,2,256]{2,1,0:T(2,128)(2,1)}), bf16[128,2,256]{2,1,0:T(2,128)(2,1)S(1)}, u32[]{:S(2)}, u32[]{:S(2)}) async-start(bf16[128,2,256]{2,1,0:T(2,128)(2,1)} %convert_element_type.215), calls=%async_computation.4 | async-start | bytes 262144 | tf_op jit(solution)/shard_map/all_to_all | solution.py:189
  189.6 7.6 %collective-permute-start.3 = (bf16[256,256]{1,0:T(8,128)(2,1)S(1)}, bf16[256,256]{1,0:T(8,128)(2,1)S(1)}, u32[]{:S(2)}, u32[]{:S(2)}) collective-permute-start(bf16[256,256]{1,0:T(8,128)(2,1)S(1)} %convert_element_type.217), channel_id=1, source_target_pairs={{128,0},{256,128},{384,256},{129,1},{257,129},{385,257},{130,2},{2... | collective-permute-start | bytes 393224 | tf_op jit(solution)/shard_map/ppermute | solution.py:15
  200.7 23.7 %all-to-all-start.5 = ((bf16[128,2,256]{2,1,0:T(2,128)(2,1)}), bf16[128,2,256]{2,1,0:T(2,128)(2,1)S(1)}, u32[]{:S(2)}, u32[]{:S(2)}) async-start(bf16[128,2,256]{2,1,0:T(2,128)(2,1)} %convert_element_type.221), calls=%async_computation.5 | async-start | bytes 262144 | tf_op jit(solution)/shard_map/all_to_all | solution.py:189
  226.7 6.6 %collective-permute-start.4 = (bf16[256,256]{1,0:T(8,128)(2,1)S(1)}, bf16[256,256]{1,0:T(8,128)(2,1)S(1)}, u32[]{:S(2)}, u32[]{:S(2)}) collective-permute-start(bf16[256,256]{1,0:T(8,128)(2,1)S(1)} %convert_element_type.223), channel_id=1, source_target_pairs={{128,0},{256,128},{384,256},{129,1},{257,129},{385,257},{130,2},{2... | collective-permute-start | bytes 393224 | tf_op jit(solution)/shard_map/ppermute | solution.py:15
  236.7 24.1 %all-to-all-start.6 = ((bf16[128,2,256]{2,1,0:T(2,128)(2,1)}), bf16[128,2,256]{2,1,0:T(2,128)(2,1)S(1)}, u32[]{:S(2)}, u32[]{:S(2)}) async-start(bf16[128,2,256]{2,1,0:T(2,128)(2,1)} %convert_element_type.227), calls=%async_computation.6 | async-start | bytes 262144 | tf_op jit(solution)/shard_map/all_to_all | solution.py:189
  263.1 6.6 %collective-permute-start.5 = (bf16[256,256]{1,0:T(8,128)(2,1)S(1)}, bf16[256,256]{1,0:T(8,128)(2,1)S(1)}, u32[]{:S(2)}, u32[]{:S(2)}) collective-permute-start(bf16[256,256]{1,0:T(8,128)(2,1)S(1)} %convert_element_type.229), channel_id=1, source_target_pairs={{128,0},{256,128},{384,256},{129,1},{257,129},{385,257},{130,2},{2... | collective-permute-start | bytes 393224 | tf_op jit(solution)/shard_map/ppermute | solution.py:15
  273.0 344.3 %all-to-all-start.7 = ((bf16[128,2,256]{2,1,0:T(2,128)(2,1)}), bf16[128,2,256]{2,1,0:T(2,128)(2,1)S(1)}, u32[]{:S(2)}, u32[]{:S(2)}) async-start(bf16[128,2,256]{2,1,0:T(2,128)(2,1)} %convert_element_type.233), calls=%async_computation.7 | async-start | bytes 262144 | tf_op jit(solution)/shard_map/all_to_all | solution.py:189
  280.9 334.8 %all-reduce.2.cloned.1.call-start = ((), (), s32[]{:S(2)}) async-start(), calls=%async_computation.8 | async-start | bytes 524288 | tf_op jit(solution)/shard_map/psum | solution.py:198
Sparse Core Ops, SparseCore 0:
  285.8 329.8 all-reduce.1
where the time goes:
time: 636 us; the launch traced here: 628 us
  blocking collectives  295 us (46%)
  waiting for transfers between devices  178 us (28%)
  starting transfers between devices  75.7 us (12%)
  local copies, waits for them, and re-layouts  22 us (3%)
  matrix products  21.6 us (3%)
  other arithmetic  19 us (3%)
  between operations  15.6 us (2%)
    psum x1, blocking collectives, on_device(): grad_weight, grad_gain = lax.psum((grad_weight, grad_gain), 'cells')  247 us
    psum x1, waiting for transfers between devices, on_device(): grad_weight, grad_gain = lax.psum((grad_weight, grad_gain), 'cells')  84 us
    all_to_all x2, blocking collectives, on_device(): lax.all_to_all(jnp.where(graph[1], picked, jnp.zeros_like(picked)), 'cell...  47.9 us
    all_to_all x4, waiting for transfers between devices, on_device(): lax.all_to_all(far_part, 'cells', split_axis=0, concat_axis=0, tiled=True)  43.9 us
    all_to_all x4, starting transfers between devices, on_device(): lax.all_to_all(far_part, 'cells', split_axis=0, concat_axis=0, tiled=True)  31.1 us
    all_to_all x2, starting transfers between devices, on_device(): lax.all_to_all(jnp.where(graph[1], picked, jnp.zeros_like(picked)), 'cell...  28.6 us
    all_to_all x2, waiting for transfers between devices, on_device(): lax.all_to_all(jnp.where(graph[1], picked, jnp.zeros_like(picked)), 'cell...  28.2 us
    ppermute x6, waiting for transfers between devices, passed_along(): lax.ppermute(value, axis, [(source, source + steps) for source in range(i...  22.4 us
  transfers between devices with their start and end apart: 13, of which 12 were waited for; matrix products, arithmetic and copies ran while one was open for 2% of the time, Pallas kernels for 0%

commit v1 on v0

v1 whole, which is shorter than its diff:
```python
import functools
import math

import jax
import jax.numpy as jnp
from jax import lax
from jax.experimental import pallas as pl
from jax.experimental.pallas import tpu as pltpu
from jax.sharding import PartitionSpec as P

EPS = 1e-05
COEF = 0.7978845608028654
CUBIC = 0.044715
LAYERS = 4
D = 256
ROWS = 256
OWNERS = 128
BLK = 128
BF = jnp.bfloat16
F32 = jnp.float32
MESH = pl.DeviceIdType.MESH
SCALE = 1.0 / math.sqrt(OWNERS * ROWS)


def mm(a, b):
    return jnp.dot(a, b, preferred_element_type=F32)


def mm_nt(a, b):
    return lax.dot_general(a, b, (((1,), (1,)), ((), ())), preferred_element_type=F32)


def mm_tn(a, b):
    return lax.dot_general(a, b, (((0,), (0,)), ((), ())), preferred_element_type=F32)


def turned(tile):
    rows = []
    for i in range(2):
        rows.append(
            jnp.concatenate(
                [tile[j * BLK : (j + 1) * BLK, i * BLK : (i + 1) * BLK].T for j in range(2)], axis=1
            )
        )
    return jnp.concatenate(rows, axis=0)


def kernel(
    feats,
    weight,
    near,
    far,
    cot,
    meta,
    out_x,
    out_g,
    out_w,
    out_gg,
    xs,
    gs,
    ws,
    near_here,
    far_here,
    meta_here,
    meta_all,
    pick,
    pick_t,
    adj,
    adj_t,
    halo,
    halo_t,
    sent,
    got,
    normed,
    slopes,
    inverse,
    acts,
    upgrad,
    wg_out,
    wg_in,
    zb_out,
    zb_in,
    wc_out,
    gg_out,
    gg_in,
    ggz_out,
    ggz_in,
    filler,
    sem_rel_send,
    sem_rel,
    sem_w_send,
    sem_w,
    sem_m_send,
    sem_m,
    sem_send,
    sem_got,
    sem_a_send,
    sem_a,
    sem_b_send,
    sem_b,
    sem_c_send,
    sem_c,
    sem_gg_send,
    sem_gg,
    sem_ggz_send,
    sem_ggz,
    sem_o_send,
    sem_o,
):
    x = lax.axis_index("segment")
    q = lax.axis_index("cells")
    z = q // 8
    wv = q % 8
    y = wv // 2
    core = wv % 2
    blk = z // 4
    zl = z % 4
    me = (4 * x + zl) * 8 + wv
    diag = x == blk
    not_diag = x != blk

    def dev(xx, zz, ww):
        return (xx, (4 * blk + zz) * 8 + ww)

    def remote(src, dst, send, recv, device):
        return pltpu.make_async_remote_copy(
            src, dst, send, recv, device_id=device, device_id_type=MESH
        )

    def wait_for(ref, sem):
        pltpu.make_async_copy(ref, ref, sem).wait()

    barrier = pltpu.get_barrier_semaphore()

    @pl.when(not_diag)
    def _():
        for xx in range(4):
            pl.semaphore_signal(
                barrier, inc=1, device_id=(xx, (4 * x + zl) * 8 + wv), device_id_type=MESH
            )

    def greet(i, carry):
        k = 127 - i
        xx = (x + k // 32) % 4
        zz = (zl + (k // 8) % 4) % 4
        ww = (wv + k % 8) % 8
        pl.semaphore_signal(barrier, inc=1, device_id=dev(xx, zz, ww), device_id_type=MESH)
        return carry

    lax.fori_loop(0, 127, greet, 0)
    pl.semaphore_wait(barrier, 130)

    def relocate(src, dst, rows, k):
        part = src.at[pl.ds(rows * x, rows)]
        there = dst.at[pl.ds(rows * x, rows)]
        for bb in range(4):

            @pl.when(jnp.logical_and(diag, blk == bb))
            def _():
                pltpu.make_async_copy(part, there, sem_rel.at[k]).start()

            @pl.when(jnp.logical_not(jnp.logical_and(diag, blk == bb)))
            def _():
                remote(
                    part,
                    there,
                    sem_rel_send.at[k],
                    sem_rel.at[k],
                    (blk, (4 * bb + zl) * 8 + wv),
                ).start()

    def relocated(src, rows, k):
        @pl.when(diag)
        def _():
            wait_for(src.at[pl.ds(0, 3 * rows)], sem_rel_send.at[k])

        @pl.when(not_diag)
        def _():
            wait_for(src.at[pl.ds(0, 4 * rows)], sem_rel_send.at[k])

    @pl.when(diag)
    def _():
        for bb in range(4):

            @pl.when(blk == bb)
            def _():
                pltpu.make_async_copy(meta, meta_here, sem_rel.at[4]).start()

            @pl.when(blk != bb)
            def _():
                remote(
                    meta,
                    meta_here,
                    sem_rel_send.at[4],
                    sem_rel.at[4],
                    (blk, (4 * bb + zl) * 8 + wv),
                ).start()

    relocate(feats, xs.at[0], 64, 0)
    relocate(near, near_here, 128, 1)
    relocate(far, far_here, 64, 2)
    for dx in (2, 1, 3):
        remote(meta, meta_all.at[x], sem_m_send, sem_m, ((x + dx) % 4, q)).start()
    pltpu.make_async_copy(meta, meta_all.at[x], sem_m).start()

    def share_weights():
        for l in range(LAYERS):

            @pl.when(x == l)
            def _():
                for dx in (2, 1, 3):
                    remote(
                        weight, ws.at[l], sem_w_send, sem_w.at[l], ((x + dx) % 4, q)
                    ).start()
                pltpu.make_async_copy(weight, ws.at[l], sem_w.at[l]).start()

    def send_all(r, matrix, source):
        for dx in (2, 1, 3, 0):
            xx = (x + dx) % 4
            rows = mm(matrix[pl.ds(pl.multiple_of(64 * xx, 64), 64), :], source)
            sent[r, pl.ds(32 * xx, 32)] = rows.astype(BF).reshape(32, 2, D)

            def to_z(i, carry):
                zz = lax.rem(zl + 3 - i, 4)
                for dy in (2, 1, 3, 0):
                    for dc in (1, 0):
                        ww = ((y + dy) % 4) * 2 + (core + dc) % 2
                        v = (4 * xx + zz) * 8 + ww
                        if dx == 0 and dy == 0 and dc == 0:

                            @pl.when(v != me)
                            def _():
                                remote(
                                    sent.at[r, v],
                                    got.at[r, me],
                                    sem_send.at[r],
                                    sem_got.at[r],
                                    dev(xx, zz, ww),
                                ).start()

                            @pl.when(v == me)
                            def _():
                                pltpu.make_async_copy(
                                    sent.at[r, v], got.at[r, v], sem_got.at[r]
                                ).start()
                        else:
                            remote(
                                sent.at[r, v],
                                got.at[r, me],
                                sem_send.at[r],
                                sem_got.at[r],
                                dev(xx, zz, ww),
                            ).start()
                return carry

            lax.fori_loop(0, 4, to_z, 0)

    def receive(r):
        wait_for(got.at[r], sem_got.at[r])
        return got[r].reshape(OWNERS * 2, D)

    def emit(value, out, kind, l):
        @pl.when(jnp.logical_and(diag, x == l))
        def _():
            pltpu.make_async_copy(value, out, sem_o.at[kind]).start()

        @pl.when(jnp.logical_and(diag, x != l))
        def _():
            remote(value, out, sem_o_send.at[kind, l], sem_o.at[kind], (l, q)).start()

    wait_for(meta_here, sem_rel.at[4])
    targets = meta_here[0:1, :]
    rows_iota = lax.broadcasted_iota(jnp.int32, (ROWS, 2 * OWNERS), 0).astype(F32)
    hot = jnp.where(rows_iota == targets, 1.0, 0.0)
    pick_t[...] = hot.astype(BF)
    pick[...] = turned(hot).astype(BF)
    wait_for(xs.at[0], sem_rel.at[0])

    def build_adjacency():
        wait_for(near_here, sem_rel.at[1])
        wait_for(far_here, sem_rel.at[2])

        def entry(k):
            return meta_here[1:2, k : k + 1]

        for listed, base, live_at, shift, values, target, target_t in (
            (4, 0, 12, 0, near_here, adj, adj_t),
            (2, 8, 13, 2, far_here, halo, halo_t),
        ):
            tiles = [values[i * BLK : (i + 1) * BLK, :].astype(F32) for i in range(listed)]
            for rb in range(2):
                for cb in range(2):
                    total = jnp.zeros((BLK, BLK), F32)
                    for i in range(listed):
                        hit = jnp.where(
                            jnp.logical_and(
                                jnp.logical_and(
                                    entry(base + 2 * i) == float(rb),
                                    entry(base + 2 * i + 1) == float(cb + shift),
                                ),
                                entry(live_at) > float(i),
                            ),
                            1.0,
                            0.0,
                        )
                        total = total + tiles[i] * hit
                    target[rb * BLK : (rb + 1) * BLK, cb * BLK : (cb + 1) * BLK] = total.astype(BF)
                    target_t[cb * BLK : (cb + 1) * BLK, rb * BLK : (rb + 1) * BLK] = (
                        total.T.astype(BF)
                    )

    def gain_of(l):
        return meta_all[l, 2:3, :]

    def norm_of(total):
        inv = lax.rsqrt(jnp.mean(total * total, axis=-1, keepdims=True) + EPS)
        return inv, total * inv

    def inner_of(v):
        return jnp.tanh(COEF * (v + CUBIC * v * v * v))

    def slope_of(v, inner):
        return 0.5 * (1.0 + inner) + 0.5 * v * (1.0 - inner * inner) * COEF * (
            1.0 + 3.0 * CUBIC * v * v
        )

    for l in range(LAYERS):
        send_all(l, pick, xs[l])
        if l == 0:
            relocate(cot, gs.at[LAYERS], 64, 3)
            share_weights()
            build_adjacency()
            wait_for(meta_all, sem_m)
        if l > 0:
            emit(xs.at[l], out_x, 0, l - 1)
            v = normed[l - 1] * gain_of(l - 1)
            slopes[l - 1] = slope_of(v, inner_of(v))
        wait_for(ws.at[l], sem_w.at[l])
        if l == LAYERS - 1:
            wait_for(gs.at[LAYERS], sem_rel.at[3])
            upgrad[...] = mm_nt(gs[LAYERS], ws[l])
        own = mm(adj[...], xs[l])
        total = own + mm(halo[...], receive(l))
        inv, nh = norm_of(total)
        v = nh * gain_of(l)
        inner = inner_of(v)
        inverse[l] = jnp.broadcast_to(inv, (ROWS, BLK))
        normed[l] = nh
        acts[l] = (0.5 * v * (1.0 + inner)).astype(BF)
        if l < LAYERS - 1:
            xs[l + 1] = (xs[l].astype(F32) + mm(acts[l], ws[l])).astype(BF)
        else:
            slopes[l] = slope_of(v, inner)

    def tiles_out(l):
        partial = mm_tn(acts[l], gs[l + 1]).astype(BF)
        for i in range(32):
            rt, ct = i // 2, i % 2
            wg_out[l, i] = partial[16 * rt : 16 * rt + 16, BLK * ct : BLK * ct + BLK]
        here = x * 8 + wv

        def to_x(i, carry):
            xx = (x + 3 - i) % 4
            for dw in range(8):
                ww = (wv + dw) % 8
                there = xx * 8 + ww
                if dw == 0:

                    @pl.when(there == here)
                    def _():
                        pltpu.make_async_copy(
                            wg_out.at[l, there], wg_in.at[l, here], sem_a.at[l]
                        ).start()

                    @pl.when(there != here)
                    def _():
                        remote(
                            wg_out.at[l, there],
                            wg_in.at[l, here],
                            sem_a_send.at[l],
                            sem_a.at[l],
                            dev(xx, zl, ww),
                        ).start()
                else:
                    remote(
                        wg_out.at[l, there],
                        wg_in.at[l, here],
                        sem_a_send.at[l],
                        sem_a.at[l],
                        dev(xx, zl, ww),
                    ).start()
            return carry

        lax.fori_loop(0, 4, to_x, 0)

    def tiles_z(l):
        wait_for(wg_in.at[l], sem_a.at[l])
        total = wg_in[l, 0].astype(F32)
        for i in range(1, 32):
            total = total + wg_in[l, i].astype(F32)
        zb_out[l] = total
        for dz in (3, 2, 1):
            remote(
                zb_out.at[l],
                zb_in.at[l, zl],
                sem_b_send.at[l],
                sem_b.at[l],
                dev(x, (zl + dz) % 4, wv),
            ).start()
        pltpu.make_async_copy(zb_out.at[l], zb_in.at[l, zl], sem_b.at[l]).start()

    def tiles_home(l):
        wait_for(zb_in.at[l], sem_b.at[l])
        wc_out[l] = (zb_in[l, 0] + zb_in[l, 1] + zb_in[l, 2] + zb_in[l, 3]) * SCALE
        place = out_w.at[
            pl.ds(pl.multiple_of(16 * (4 * x + wv // 2), 16), 16),
            pl.ds(pl.multiple_of(BLK * (wv % 2), BLK), BLK),
        ]
        for dw in (4, 5, 3, 2, 6, 7, 1, 0):
            ww = (wv + dw) % 8
            if dw == 0:

                @pl.when(x == l)
                def _():
                    pltpu.make_async_copy(wc_out.at[l], place, sem_c).start()

                @pl.when(x != l)
                def _():
                    remote(wc_out.at[l], place, sem_c_send.at[l], sem_c, dev(l, zl, ww)).start()
            else:
                remote(wc_out.at[l], place, sem_c_send.at[l], sem_c, dev(l, zl, ww)).start()

    def gains_out(l):
        for dw in (4, 5, 3, 2, 6, 7, 1, 0):
            ww = (wv + dw) % 8
            place = gg_in.at[x * 8 + wv]
            if dw == 0:

                @pl.when(x == l)
                def _():
                    pltpu.make_async_copy(gg_out.at[l], place, sem_gg).start()

                @pl.when(x != l)
                def _():
                    remote(gg_out.at[l], place, sem_gg_send.at[l], sem_gg, dev(l, zl, ww)).start()
            else:
                remote(gg_out.at[l], place, sem_gg_send.at[l], sem_gg, dev(l, zl, ww)).start()

    for l in reversed(range(LAYERS)):
        r = 2 * LAYERS - 1 - l
        if l < LAYERS - 1:
            if l == 0:
                tiles_out(l)
            upgrad[...] = mm_nt(gs[l + 1], ws[l])
        nh = normed[l]
        m = upgrad[...] * slopes[l]
        s = m * gain_of(l)
        t = jnp.mean(s * nh, axis=-1, keepdims=True)
        down = (inverse[l][:, 0:1] * (s - nh * t)).astype(BF)
        send_all(r, halo_t, down)
        gg_out[l] = jnp.sum(m * nh, axis=0, keepdims=True)
        gains_out(l)
        if l == LAYERS - 1:
            xs[LAYERS] = (xs[l].astype(F32) + mm(acts[l], ws[l])).astype(BF)
            emit(xs.at[LAYERS], out_x, 0, l)
        else:
            emit(gs.at[l + 1], out_g, 1, l + 1)
        if l > 0:
            tiles_out(l)
        own = mm(adj_t[...], down)
        if l + 1 < LAYERS:
            tiles_z(l + 1)
        if l + 2 < LAYERS:
            tiles_home(l + 2)
        if l == 0:
            tiles_home(1)
            tiles_z(0)
        gs[l] = (gs[l + 1].astype(F32) + own + mm(pick_t[...], receive(r))).astype(BF)

    emit(gs.at[0], out_g, 1, 0)
    wait_for(gg_in, sem_gg)
    ggz_out[...] = jnp.sum(gg_in[...], axis=0)
    for dz in (3, 2, 1):
        remote(
            ggz_out, ggz_in.at[zl], sem_ggz_send, sem_ggz, dev(x, (zl + dz) % 4, wv)
        ).start()
    pltpu.make_async_copy(ggz_out, ggz_in.at[zl], sem_ggz).start()
    tiles_home(0)
    wait_for(ggz_in, sem_ggz)
    out_gg[...] = jnp.sum(ggz_in[...], axis=0) * SCALE

    wait_for(out_x, sem_o.at[0])
    wait_for(out_g, sem_o.at[1])
    wait_for(out_w, sem_c)
    relocated(feats, 64, 0)
    relocated(near, 128, 1)
    relocated(far, 64, 2)
    relocated(cot, 64, 3)

    @pl.when(diag)
    def _():
        wait_for(meta_all.at[pl.ds(0, 3)], sem_rel_send.at[4])

    wait_for(meta_all.at[pl.ds(0, 3)], sem_m_send)
    wait_for(ws.at[pl.ds(0, 3)], sem_w_send)
    for r in range(2 * LAYERS):
        wait_for(sent.at[r, pl.ds(0, OWNERS - 1)], sem_send.at[r])
    for l in range(LAYERS):
        wait_for(wg_in.at[l, pl.ds(0, 31)], sem_a_send.at[l])
        wait_for(zb_in.at[l, pl.ds(0, 3)], sem_b_send.at[l])

        @pl.when(x == l)
        def _():
            wait_for(filler.at[pl.ds(0, 7)], sem_c_send.at[l])
            wait_for(gg_in.at[pl.ds(0, 7)], sem_gg_send.at[l])

        @pl.when(x != l)
        def _():
            wait_for(filler, sem_c_send.at[l])
            wait_for(gg_in.at[pl.ds(0, 8)], sem_gg_send.at[l])

        @pl.when(jnp.logical_and(diag, x != l))
        def _():
            wait_for(gs.at[l], sem_o_send.at[0, l])
            wait_for(gs.at[l], sem_o_send.at[1, l])

    wait_for(ggz_in.at[pl.ds(0, 3)], sem_ggz_send)


def on_device(
    feats,
    weights,
    gains,
    send_rows,
    send_count,
    local_index,
    halo_index,
    block_count,
    local_vals,
    halo_vals,
    cotangent,
):
    live = jnp.arange(2)[None, :] < send_count[0, 0][:, None]
    targets = jnp.where(live, send_rows[0, 0], -1).astype(F32).reshape(1, 2 * OWNERS)
    lists = jnp.concatenate(
        [local_index.reshape(-1), halo_index.reshape(-1), block_count.reshape(-1)]
    ).astype(F32)
    lists = jnp.pad(lists, (0, D - lists.shape[0]))[None]
    meta = jnp.concatenate([targets, lists, gains, jnp.zeros((5, D), F32)], axis=0)
    any_spec = pl.BlockSpec(memory_space=pl.ANY)
    vmem_spec = pl.BlockSpec(memory_space=pltpu.VMEM)
    dma = pltpu.SemaphoreType.DMA
    out_x, out_g, out_w, out_gg = pl.pallas_call(
        kernel,
        out_shape=(
            jax.ShapeDtypeStruct((ROWS, D), BF),
            jax.ShapeDtypeStruct((ROWS, D), BF),
            jax.ShapeDtypeStruct((D, D), F32),
            jax.ShapeDtypeStruct((1, D), F32),
        ),
        in_specs=[any_spec] * 6,
        out_specs=(any_spec, any_spec, any_spec, vmem_spec),
        scratch_shapes=[
            pltpu.VMEM((LAYERS + 1, ROWS, D), BF),
            pltpu.VMEM((LAYERS + 1, ROWS, D), BF),
            pltpu.VMEM((LAYERS, D, D), BF),
            pltpu.VMEM((4 * BLK, BLK), BF),
            pltpu.VMEM((2 * BLK, BLK), BF),
            pltpu.VMEM((8, D), F32),
            pltpu.VMEM((LAYERS, 8, D), F32),
            pltpu.VMEM((2 * OWNERS, ROWS), BF),
            pltpu.VMEM((ROWS, 2 * OWNERS), BF),
            pltpu.VMEM((ROWS, ROWS), BF),
            pltpu.VMEM((ROWS, ROWS), BF),
            pltpu.VMEM((ROWS, 2 * OWNERS), BF),
            pltpu.VMEM((2 * OWNERS, ROWS), BF),
            pltpu.VMEM((2 * LAYERS, OWNERS, 2, D), BF),
            pltpu.VMEM((2 * LAYERS, OWNERS, 2, D), BF),
            pltpu.VMEM((LAYERS, ROWS, D), F32),
            pltpu.VMEM((LAYERS, ROWS, D), F32),
            pltpu.VMEM((LAYERS, ROWS, BLK), F32),
            pltpu.VMEM((LAYERS, ROWS, D), BF),
            pltpu.VMEM((ROWS, D), F32),
            pltpu.VMEM((LAYERS, 32, 16, BLK), BF),
            pltpu.VMEM((LAYERS, 32, 16, BLK), BF),
            pltpu.VMEM((LAYERS, 16, BLK), F32),
            pltpu.VMEM((LAYERS, 4, 16, BLK), F32),
            pltpu.VMEM((LAYERS, 16, BLK), F32),
            pltpu.VMEM((LAYERS, 1, D), F32),
            pltpu.VMEM((32, 1, D), F32),
            pltpu.VMEM((1, D), F32),
            pltpu.VMEM((4, 1, D), F32),
            pltpu.VMEM((8, 16, BLK), F32),
            dma((5,)),
            dma((5,)),
            dma,
            dma((LAYERS,)),
            dma,
            dma,
            dma((2 * LAYERS,)),
            dma((2 * LAYERS,)),
            dma((LAYERS,)),
            dma((LAYERS,)),
            dma((LAYERS,)),
            dma((LAYERS,)),
            dma((LAYERS,)),
            dma,
            dma((LAYERS,)),
            dma,
            dma,
            dma,
            dma((2, LAYERS)),
            dma((2,)),
        ],
        compiler_params=pltpu.CompilerParams(
            collective_id=0, has_side_effects=True, vmem_limit_bytes=48 * 1024 * 1024
        ),
    )(
        feats[0],
        weights[0],
        local_vals.reshape(4 * BLK, BLK),
        halo_vals.reshape(2 * BLK, BLK),
        cotangent[0],
        meta,
    )
    return out_x[None, None], out_g[None, None], out_w[None], out_gg


def solution(mesh):
    in_specs = (
        P(None, "cells", None),
        P("segment", None, None),
        P("segment", None),
        P(None, "cells", None, None),
        P(None, "cells", None),
        P(None, "cells", None, None),
        P(None, "cells", None, None),
        P(None, "cells", None),
        P(None, "cells", None, None),
        P(None, "cells", None, None),
        P(None, "cells", None),
    )
    out_specs = (
        P("segment", None, "cells", None),
        P("segment", None, "cells", None),
        P("segment", None, None),
        P("segment", None),
    )
    return jax.shard_map(
        on_device, mesh=mesh, in_specs=in_specs, out_specs=out_specs, check_vma=False
    )
```

time: 636 us -> 115 us (0.18); the launches traced: 628 us -> 115 us
  blocking collectives: 295 us -> 0 us
  waiting for transfers between devices: 178 us -> 0 us
  Pallas kernels: 0 us -> 104 us
  starting transfers between devices: 75.7 us -> 0 us
  matrix products: 21.6 us -> 0 us
  other arithmetic: 19 us -> 1.55 us
  between operations: 15.6 us -> 0.69 us
  local copies, waits for them, and re-layouts: 22 us -> 8.79 us
    psum x1 -> x0, blocking collectives: 247 us -> none  [on_device(): grad_weight, grad_gain = lax.psum((grad_weight, grad_gain), 'cells')]
    pallas_call x0 -> x1, Pallas kernels: none -> 104 us  [on_device(): pl.pallas_call(kernel, out_shape=(jax.ShapeDtypeStruct((ROWS, D), BF), ja...]
    psum x1 -> x0, waiting for transfers between devices: 84 us -> none  [on_device(): grad_weight, grad_gain = lax.psum((grad_weight, grad_gain), 'cells')]
    all_to_all x6 -> x0, waiting for transfers between devices: 72 us -> none  [the longest x4 43.9 us: on_device(): lax.all_to_all(far_part, 'cells', split_axis=0, concat_axis=0, tiled=True)]
    all_to_all x6 -> x0, starting transfers between devices: 59.6 us -> none  [the longest x4 31.1 us: on_device(): lax.all_to_all(far_part, 'cells', split_axis=0, concat_axis=0, tiled=True)]
    all_to_all x2 -> x0, blocking collectives: 47.9 us -> none  [on_device(): lax.all_to_all(jnp.where(graph[1], picked, jnp.zeros_like(picked)), 'cell...]
    ppermute x6 -> x0, waiting for transfers between devices: 22.4 us -> none  [passed_along(): lax.ppermute(value, axis, [(source, source + steps) for source in range(i...]
    dot_general x44 -> x0, matrix products: 21.6 us -> none  [the longest x8 6.37 us: block_transpose(): jnp.einsum('cb,bjd->cjd', select, product, precision=lax.Precision.HIGHEST)]
  transfers between devices with their start and end apart: 13 -> 0, of which waited for: 12 -> 0; matrix products, arithmetic and copies ran while one was open for 2% -> 0% of each run, Pallas kernels for 0% -> 0%
where the time goes in v1:
time: 115 us
  Pallas kernels  104 us (90%)
  local copies, waits for them, and re-layouts  8.79 us (8%)
  other arithmetic  1.55 us (1%)
    pallas_call x1, Pallas kernels, on_device(): pl.pallas_call(kernel, out_shape=(jax.ShapeDtypeStruct((ROWS, D), BF), ja...  104 us
    unnamed x18, local copies, waits for them, and re-layouts  7.54 us

profile of v1, /device:TPU:1, one launch (start us, length us, event | category | flops | bytes accessed | tf_op | source)
XLA Modules:
  0.0 115.1 jit_solution(2898788603897275624)
XLA Ops:
  0.6 0.0 copy-start
  0.6 0.8 reshape.63
  1.4 0.1 pad.8.clone
  1.5 0.8 copy.18
  2.3 0.1 reshape.62
  2.4 0.7 add_convert_fusion
  3.1 0.7 iota_compare_fusion
  3.8 0.1 lt.29
  4.0 0.0 copy-start.4
  4.0 0.8 copy.17
  4.8 0.1 squeeze.15
  5.0 0.0 copy-start.5
  5.0 0.7 copy-done.5
  5.7 0.1 maximum_maximum_fusion.meta
  5.7 0.0 copy-done
  5.7 0.0 copy-done.4
  5.7 0.0 copy-start.1
  5.7 0.9 copy-done.1
  6.6 0.0 copy-start.2
  6.6 0.9 copy-done.2
  7.5 0.0 copy-start.3
  7.5 0.9 copy-done.3
  8.4 104.1 %shard_map.138 = (bf16[256,256]{1,0:T(8,128)(2,1)S(1)}, bf16[256,256]{1,0:T(8,128)(2,1)S(1)}, f32[256,256]{1,0:T(8,128)S(1)}, f32[1,256]{1,0:T(1,128)S(1)}) custom-call(bf16[256,256]{1,0:T(8,128)(2,1)S(1)} %bitcast.16, bf16[256,256]{1,0:T(8,128)(2,1)S(1)} %bitcast.17, bf16[512,128]{1,0:T(8,128)(2,1)S(1)} %bitcast.18, bf16[256,128]{1,0:T(8,128)(2,1)S(1)} %bitcast.20, ...), custom_call_target="tpu_custom_call" | custom-call | tf_op jit(solution)/shard_map/pallas_call | solution.py:553
  112.6 0.7 copy.23
  113.2 0.7 copy.24
  113.9 0.7 copy.25
  114.6 0.6 copy.26
  (3 shorter events, 0.0 us)
Async XLA Ops:
  0.6 5.1 %copy-start = (bf16[1,256,256]{2,1,0:T(8,128)(2,1)S(1)}, bf16[1,256,256]{2,1,0:T(8,128)(2,1)}, u32[]{:S(2)}) copy-start(bf16[1,256,256]{2,1,0:T(8,128)(2,1)} %param.11) | copy-start | bytes 393220
  4.0 1.7 %copy-start.4 = (bf16[1,2,128,128]{3,2,1,0:T(8,128)(2,1)S(1)}, bf16[1,2,128,128]{3,2,1,0:T(8,128)(2,1)}, u32[]{:S(2)}) copy-start(bf16[1,2,128,128]{3,2,1,0:T(8,128)(2,1)} %param.20) | copy-start | bytes 196612
  5.0 0.7 copy-start.5
  5.7 0.9 copy-start.1
  6.6 0.9 copy-start.2
  7.5 0.9 copy-start.3

commit v2 on v1

--- a/solution.py
+++ b/solution.py
@@ -51,7 +51,12 @@
     near,
     far,
     cot,
-    meta,
+    rows_in,
+    count_in,
+    near_in,
+    far_in,
+    live_in,
+    gains_in,
     out_x,
     out_g,
     out_w,
@@ -61,10 +66,18 @@
     ws,
     near_here,
     far_here,
+    rows_v,
+    count_v,
+    near_v,
+    far_v,
+    live_v,
+    gains_v,
+    meta,
     meta_here,
     meta_all,
     pick,
     pick_t,
+    pick_home_t,
     adj,
     adj_t,
     halo,
@@ -83,9 +96,10 @@
     wc_out,
     gg_out,
     gg_in,
-    ggz_out,
-    ggz_in,
+    base_out,
+    base_in,
     filler,
+    sem_in,
     sem_rel_send,
     sem_rel,
     sem_w_send,
@@ -102,8 +116,8 @@
     sem_c,
     sem_gg_send,
     sem_gg,
-    sem_ggz_send,
-    sem_ggz,
+    sem_base_send,
+    sem_base,
     sem_o_send,
     sem_o,
 ):
@@ -115,7 +129,13 @@
     core = wv % 2
     blk = z // 4
     zl = z % 4
-    me = (4 * x + zl) * 8 + wv
+
+    def seat(xx, zz):
+        aside = jnp.where(lax.rem(blk + 4 - xx, 4) == 2, 1, 0)
+        return zz + aside * (1 - 2 * lax.rem(zz, 2))
+
+    zo = seat(x, zl)
+    me = (4 * x + zo) * 8 + wv
     diag = x == blk
     not_diag = x != blk
 
@@ -130,30 +150,73 @@
     def wait_for(ref, sem):
         pltpu.make_async_copy(ref, ref, sem).wait()
 
+    small = [
+        pltpu.make_async_copy(there, here, sem_in.at[i])
+        for i, (there, here) in enumerate(
+            (
+                (rows_in, rows_v),
+                (count_in, count_v),
+                (near_in, near_v),
+                (far_in, far_v),
+                (live_in, live_v),
+                (gains_in, gains_v),
+            )
+        )
+    ]
+    for copy in small:
+        copy.start()
+
+    seg_of = [lax.rem(x + i, 4) for i in range(4)]
+    upper = zl // 2
+    z_near = zl + 1 - 2 * lax.rem(zl, 2)
+    z_by_distance = (3 - 3 * upper, 2 - upper, z_near, zl)
+    base_of = [(4 * blk + zz) * 8 for zz in z_by_distance]
+    lane_of = {
+        (dy, dc): lax.rem(y + dy, 4) * 2 + (lax.rem(core + 1, 2) if dc else core)
+        for dy in range(4)
+        for dc in range(2)
+    }
+    in_order = sorted(
+        ((i, dy, dc) for i in range(4) for dy in range(4) for dc in range(2)),
+        key=lambda t: -((2.5, 1.5, 1.0, 0.0)[t[0]] + (0, 1, 2, 1)[t[1]] + 0.1 * t[2]),
+    )
+
     barrier = pltpu.get_barrier_semaphore()
 
     @pl.when(not_diag)
     def _():
         for xx in range(4):
             pl.semaphore_signal(
-                barrier, inc=1, device_id=(xx, (4 * x + zl) * 8 + wv), device_id_type=MESH
+                barrier, inc=1, device_id=(xx, (4 * x + zo) * 8 + wv), device_id_type=MESH
             )
 
-    def greet(i, carry):
-        k = 127 - i
-        xx = (x + k // 32) % 4
-        zz = (zl + (k // 8) % 4) % 4
-        ww = (wv + k % 8) % 8
-        pl.semaphore_signal(barrier, inc=1, device_id=dev(xx, zz, ww), device_id_type=MESH)
-        return carry
-
-    lax.fori_loop(0, 127, greet, 0)
+    for dx in (2, 1, 3, 0):
+        for i, dy, dc in in_order:
+            if (dx, i, dy, dc) != (0, 3, 0, 0):
+                pl.semaphore_signal(
+                    barrier,
+                    inc=1,
+                    device_id=(seg_of[dx], base_of[i] + lane_of[dy, dc]),
+                    device_id_type=MESH,
+                )
+
+    for copy in small:
+        copy.wait()
+    meta[...] = jnp.zeros_like(meta)
+    for k in range(2):
+        wanted = jnp.where(count_v[...] > k, rows_v[k : k + 1, :], -1)
+        meta[0:1, k * OWNERS : (k + 1) * OWNERS] = wanted.astype(F32)
+    meta[2:4, 0:4] = near_v[...].astype(F32)
+    meta[4:6, 0:2] = far_v[...].astype(F32)
+    meta[6:7, 0:2] = live_v[...].astype(F32)
+    meta[7:8, :] = gains_v[...]
     pl.semaphore_wait(barrier, 130)
 
     def relocate(src, dst, rows, k):
         part = src.at[pl.ds(rows * x, rows)]
         there = dst.at[pl.ds(rows * x, rows)]
         for bb in range(4):
+            there_z = jnp.where(lax.rem(bb + 4 - blk, 4) == 2, z_near, zl)
 
             @pl.when(jnp.logical_and(diag, blk == bb))
             def _():
@@ -166,7 +229,7 @@
                     there,
                     sem_rel_send.at[k],
                     sem_rel.at[k],
-                    (blk, (4 * bb + zl) * 8 + wv),
+                    (blk, (4 * bb + there_z) * 8 + wv),
                 ).start()
 
     def relocated(src, rows, k):
@@ -181,6 +244,7 @@
     @pl.when(diag)
     def _():
         for bb in range(4):
+            there_z = jnp.where(lax.rem(bb + 4 - blk, 4) == 2, z_near, zl)
 
             @pl.when(blk == bb)
             def _():
@@ -193,7 +257,7 @@
                     meta_here,
                     sem_rel_send.at[4],
                     sem_rel.at[4],
-                    (blk, (4 * bb + zl) * 8 + wv),
+                    (blk, (4 * bb + there_z) * 8 + wv),
                 ).start()
 
     relocate(feats, xs.at[0], 64, 0)
@@ -216,44 +280,19 @@
 
     def send_all(r, matrix, source):
         for dx in (2, 1, 3, 0):
-            xx = (x + dx) % 4
+            xx = seg_of[dx]
             rows = mm(matrix[pl.ds(pl.multiple_of(64 * xx, 64), 64), :], source)
             sent[r, pl.ds(32 * xx, 32)] = rows.astype(BF).reshape(32, 2, D)
 
-            def to_z(i, carry):
-                zz = lax.rem(zl + 3 - i, 4)
-                for dy in (2, 1, 3, 0):
-                    for dc in (1, 0):
-                        ww = ((y + dy) % 4) * 2 + (core + dc) % 2
-                        v = (4 * xx + zz) * 8 + ww
-                        if dx == 0 and dy == 0 and dc == 0:
-
-                            @pl.when(v != me)
-                            def _():
-                                remote(
-                                    sent.at[r, v],
-                                    got.at[r, me],
-                                    sem_send.at[r],
-                                    sem_got.at[r],
-                                    dev(xx, zz, ww),
-                                ).start()
-
-                            @pl.when(v == me)
-                            def _():
-                                pltpu.make_async_copy(
-                                    sent.at[r, v], got.at[r, v], sem_got.at[r]
-                                ).start()
-                        else:
-                            remote(
-                                sent.at[r, v],
-                                got.at[r, me],
-                                sem_send.at[r],
-                                sem_got.at[r],
-                                dev(xx, zz, ww),
-                            ).start()
-                return carry
-
-            lax.fori_loop(0, 4, to_z, 0)
+            for i, dy, dc in in_order:
+                cell = base_of[i] + lane_of[dy, dc]
+                v = 32 * xx + 8 * seat(xx, z_by_distance[i]) + lane_of[dy, dc]
+                if (dx, i, dy, dc) == (0, 3, 0, 0):
+                    pltpu.make_async_copy(sent.at[r, v], got.at[r, v], sem_got.at[r]).start()
+                else:
+                    remote(
+                        sent.at[r, v], got.at[r, me], sem_send.at[r], sem_got.at[r], (xx, cell)
+                    ).start()
 
     def receive(r):
         wait_for(got.at[r], sem_got.at[r])
@@ -269,48 +308,48 @@
             remote(value, out, sem_o_send.at[kind, l], sem_o.at[kind], (l, q)).start()
 
     wait_for(meta_here, sem_rel.at[4])
-    targets = meta_here[0:1, :]
-    rows_iota = lax.broadcasted_iota(jnp.int32, (ROWS, 2 * OWNERS), 0).astype(F32)
-    hot = jnp.where(rows_iota == targets, 1.0, 0.0)
-    pick_t[...] = hot.astype(BF)
-    pick[...] = turned(hot).astype(BF)
+    def placed(targets):
+        row_of = lax.broadcasted_iota(jnp.int32, (ROWS, 2 * OWNERS), 0)
+        slot_of = lax.broadcasted_iota(jnp.int32, (ROWS, 2 * OWNERS), 1)
+        hot = jnp.where(row_of.astype(F32) == targets, 1.0, 0.0).astype(BF)
+        order = jnp.where(row_of == lax.rem(slot_of, 2) * OWNERS + slot_of // 2, 1.0, 0.0)
+        return mm(hot, order.astype(BF))
+
+    at_rows = placed(meta_here[0:1, :])
+    pick_t[...] = at_rows.astype(BF)
+    pick[...] = turned(at_rows).astype(BF)
     wait_for(xs.at[0], sem_rel.at[0])
 
     def build_adjacency():
         wait_for(near_here, sem_rel.at[1])
         wait_for(far_here, sem_rel.at[2])
 
-        def entry(k):
-            return meta_here[1:2, k : k + 1]
-
-        for listed, base, live_at, shift, values, target, target_t in (
-            (4, 0, 12, 0, near_here, adj, adj_t),
-            (2, 8, 13, 2, far_here, halo, halo_t),
+        def entry(row, lane):
+            return meta_here[row : row + 1, lane : lane + 1]
+
+        near_lists = [(entry(2, i), entry(3, i)) for i in range(4)]
+        far_lists = [(entry(4 + i, 0), entry(4 + i, 1)) for i in range(2)]
+        for lists, live, shift, values, target, target_t in (
+            (near_lists, entry(6, 0), 0, near_here, adj, adj_t),
+            (far_lists, entry(6, 1), 2, far_here, halo, halo_t),
         ):
-            tiles = [values[i * BLK : (i + 1) * BLK, :].astype(F32) for i in range(listed)]
+            tiles = [values[i * BLK : (i + 1) * BLK, :].astype(F32) for i in range(len(lists))]
             for rb in range(2):
                 for cb in range(2):
                     total = jnp.zeros((BLK, BLK), F32)
-                    for i in range(listed):
-                        hit = jnp.where(
-                            jnp.logical_and(
-                                jnp.logical_and(
-                                    entry(base + 2 * i) == float(rb),
-                                    entry(base + 2 * i + 1) == float(cb + shift),
-                                ),
-                                entry(live_at) > float(i),
-                            ),
-                            1.0,
-                            0.0,
+                    for i, (row, col) in enumerate(lists):
+                        hit = jnp.logical_and(
+                            jnp.logical_and(row == float(rb), col == float(cb + shift)),
+                            live > float(i),
                         )
-                        total = total + tiles[i] * hit
+                        total = total + tiles[i] * jnp.where(hit, 1.0, 0.0)
                     target[rb * BLK : (rb + 1) * BLK, cb * BLK : (cb + 1) * BLK] = total.astype(BF)
                     target_t[cb * BLK : (cb + 1) * BLK, rb * BLK : (rb + 1) * BLK] = (
                         total.T.astype(BF)
                     )
 
     def gain_of(l):
-        return meta_all[l, 2:3, :]
+        return meta_all[l, 7:8, :]
 
     def norm_of(total):
         inv = lax.rsqrt(jnp.mean(total * total, axis=-1, keepdims=True) + EPS)
@@ -331,6 +370,10 @@
             share_weights()
             build_adjacency()
             wait_for(meta_all, sem_m)
+        if l == 1:
+            pick_home_t[...] = placed(meta[0:1, :]).astype(BF)
+        if l == 2:
+            send_all(2 * LAYERS, pick, acts[0])
         if l > 0:
             emit(xs.at[l], out_x, 0, l - 1)
             v = normed[l - 1] * gain_of(l - 1)
@@ -352,8 +395,8 @@
         else:
             slopes[l] = slope_of(v, inner)
 
-    def tiles_out(l):
-        partial = mm_tn(acts[l], gs[l + 1]).astype(BF)
+    def tiles_out(l, partial):
+        partial = partial.astype(BF)
         for i in range(32):
             rt, ct = i // 2, i % 2
             wg_out[l, i] = partial[16 * rt : 16 * rt + 16, BLK * ct : BLK * ct + BLK]
@@ -431,10 +474,10 @@
                 remote(wc_out.at[l], place, sem_c_send.at[l], sem_c, dev(l, zl, ww)).start()
 
     def gains_out(l):
-        for dw in (4, 5, 3, 2, 6, 7, 1, 0):
-            ww = (wv + dw) % 8
-            place = gg_in.at[x * 8 + wv]
-            if dw == 0:
+        place = gg_in.at[(4 * x + zl) * 8 + wv]
+        for i, dy, dc in in_order:
+            cell = base_of[i] + lane_of[dy, dc]
+            if (i, dy, dc) == (3, 0, 0):
 
                 @pl.when(x == l)
                 def _():
@@ -442,52 +485,97 @@
 
                 @pl.when(x != l)
                 def _():
-                    remote(gg_out.at[l], place, sem_gg_send.at[l], sem_gg, dev(l, zl, ww)).start()
+                    remote(gg_out.at[l], place, sem_gg_send.at[l], sem_gg, (l, cell)).start()
             else:
-                remote(gg_out.at[l], place, sem_gg_send.at[l], sem_gg, dev(l, zl, ww)).start()
+                remote(gg_out.at[l], place, sem_gg_send.at[l], sem_gg, (l, cell)).start()
+
+    def send_home(r, source):
+        rows = mm(halo_t[pl.ds(pl.multiple_of(64 * blk, 64), 64), :], source)
+        sent[r, pl.ds(32 * blk, 32)] = rows.astype(BF).reshape(32, 2, D)
+        for i, dy, dc in in_order:
+            cell = base_of[i] + lane_of[dy, dc]
+            v = 32 * blk + 8 * z_by_distance[i] + lane_of[dy, dc]
+            message = sent.at[r, v]
+            if (i, dy, dc) == (3, 0, 0):
+
+                @pl.when(x == 0)
+                def _():
+                    pltpu.make_async_copy(message, got.at[r, me], sem_got.at[r]).start()
+
+                @pl.when(x != 0)
+                def _():
+                    remote(
+                        message, got.at[r, me], sem_send.at[r], sem_got.at[r], (0, cell)
+                    ).start()
+            else:
+                remote(message, got.at[r, me], sem_send.at[r], sem_got.at[r], (0, cell)).start()
 
     for l in reversed(range(LAYERS)):
         r = 2 * LAYERS - 1 - l
         if l < LAYERS - 1:
-            if l == 0:
-                tiles_out(l)
             upgrad[...] = mm_nt(gs[l + 1], ws[l])
         nh = normed[l]
         m = upgrad[...] * slopes[l]
         s = m * gain_of(l)
         t = jnp.mean(s * nh, axis=-1, keepdims=True)
         down = (inverse[l][:, 0:1] * (s - nh * t)).astype(BF)
-        send_all(r, halo_t, down)
+        if l > 0:
+            send_all(r, halo_t, down)
+        else:
+            send_home(r, down)
+        own = mm(adj_t[...], down)
+        if l == 0:
+            base = gs[1].astype(F32) + own
+
+            @pl.when(jnp.logical_and(diag, x == 0))
+            def _():
+                base_in[...] = base
+
+            @pl.when(jnp.logical_and(diag, x != 0))
+            def _():
+                base_out[...] = base
+                remote(base_out, base_in, sem_base_send, sem_base, (0, q)).start()
+
         gg_out[l] = jnp.sum(m * nh, axis=0, keepdims=True)
         gains_out(l)
+        if l == 0:
+            tiles_z(0)
+            tiles_z(1)
+        if l == 1:
+            near_part = (gs[2].astype(F32) + own).astype(BF)
+            far_part = sent[r].reshape(2 * OWNERS, D)
+            tiles_out(
+                0, mm_tn(acts[0], near_part) + mm_tn(receive(2 * LAYERS), far_part)
+            )
+        if l > 0:
+            tiles_out(l, mm_tn(acts[l], gs[l + 1]))
         if l == LAYERS - 1:
             xs[LAYERS] = (xs[l].astype(F32) + mm(acts[l], ws[l])).astype(BF)
             emit(xs.at[LAYERS], out_x, 0, l)
         else:
             emit(gs.at[l + 1], out_g, 1, l + 1)
+        if l in (1, 2):
+            tiles_z(l + 1)
+        if l in (0, 1):
+            tiles_home(l + 2)
         if l > 0:
-            tiles_out(l)
-        own = mm(adj_t[...], down)
-        if l + 1 < LAYERS:
-            tiles_z(l + 1)
-        if l + 2 < LAYERS:
-            tiles_home(l + 2)
-        if l == 0:
-            tiles_home(1)
-            tiles_z(0)
-        gs[l] = (gs[l + 1].astype(F32) + own + mm(pick_t[...], receive(r))).astype(BF)
-
-    emit(gs.at[0], out_g, 1, 0)
+            gs[l] = (gs[l + 1].astype(F32) + own + mm(pick_t[...], receive(r))).astype(BF)
+
+    tiles_home(0)
+    tiles_home(1)
+
+    @pl.when(x == 0)
+    def _():
+        @pl.when(not_diag)
+        def _():
+            wait_for(base_in, sem_base)
+
+        spread = mm(pick_home_t[...], receive(2 * LAYERS - 1))
+        gs[0] = (base_in[...] + spread).astype(BF)
+        pltpu.make_async_copy(gs.at[0], out_g, sem_o.at[1]).start()
+
     wait_for(gg_in, sem_gg)
-    ggz_out[...] = jnp.sum(gg_in[...], axis=0)
-    for dz in (3, 2, 1):
-        remote(
-            ggz_out, ggz_in.at[zl], sem_ggz_send, sem_ggz, dev(x, (zl + dz) % 4, wv)
-        ).start()
-    pltpu.make_async_copy(ggz_out, ggz_in.at[zl], sem_ggz).start()
-    tiles_home(0)
-    wait_for(ggz_in, sem_ggz)
-    out_gg[...] = jnp.sum(ggz_in[...], axis=0) * SCALE
+    out_gg[...] = jnp.sum(gg_in[...], axis=0) * SCALE
 
     wait_for(out_x, sem_o.at[0])
     wait_for(out_g, sem_o.at[1])
@@ -503,8 +591,22 @@
 
     wait_for(meta_all.at[pl.ds(0, 3)], sem_m_send)
     wait_for(ws.at[pl.ds(0, 3)], sem_w_send)
-    for r in range(2 * LAYERS):
-        wait_for(sent.at[r, pl.ds(0, OWNERS - 1)], sem_send.at[r])
+    for r in range(2 * LAYERS + 1):
+        if r != 2 * LAYERS - 1:
+            wait_for(sent.at[r, pl.ds(0, OWNERS - 1)], sem_send.at[r])
+
+    @pl.when(x == 0)
+    def _():
+        wait_for(sent.at[0, pl.ds(0, 31)], sem_send.at[2 * LAYERS - 1])
+
+    @pl.when(x != 0)
+    def _():
+        wait_for(sent.at[0, pl.ds(0, 32)], sem_send.at[2 * LAYERS - 1])
+
+    @pl.when(jnp.logical_and(diag, x != 0))
+    def _():
+        wait_for(base_out, sem_base_send)
+
     for l in range(LAYERS):
         wait_for(wg_in.at[l, pl.ds(0, 31)], sem_a_send.at[l])
         wait_for(zb_in.at[l, pl.ds(0, 3)], sem_b_send.at[l])
@@ -512,19 +614,30 @@
         @pl.when(x == l)
         def _():
             wait_for(filler.at[pl.ds(0, 7)], sem_c_send.at[l])
-            wait_for(gg_in.at[pl.ds(0, 7)], sem_gg_send.at[l])
+            wait_for(gg_in.at[pl.ds(0, 31)], sem_gg_send.at[l])
 
         @pl.when(x != l)
         def _():
             wait_for(filler, sem_c_send.at[l])
-            wait_for(gg_in.at[pl.ds(0, 8)], sem_gg_send.at[l])
+            wait_for(gg_in.at[pl.ds(0, 32)], sem_gg_send.at[l])
 
         @pl.when(jnp.logical_and(diag, x != l))
         def _():
             wait_for(gs.at[l], sem_o_send.at[0, l])
-            wait_for(gs.at[l], sem_o_send.at[1, l])
-
-    wait_for(ggz_in.at[pl.ds(0, 3)], sem_ggz_send)
+            if l > 0:
+                wait_for(gs.at[l], sem_o_send.at[1, l])
+
+
+def settle(*refs):
+    ins = [pltpu.make_async_copy(refs[i], refs[8 + i], refs[12].at[i]) for i in range(4)]
+    outs = [pltpu.make_async_copy(refs[8 + i], refs[4 + i], refs[13].at[i]) for i in range(4)]
+    for copy in ins:
+        copy.start()
+    for copy, then in zip(ins, outs):
+        copy.wait()
+        then.start()
+    for copy in outs:
+        copy.wait()
 
 
 def on_device(
@@ -540,13 +653,7 @@
     halo_vals,
     cotangent,
 ):
-    live = jnp.arange(2)[None, :] < send_count[0, 0][:, None]
-    targets = jnp.where(live, send_rows[0, 0], -1).astype(F32).reshape(1, 2 * OWNERS)
-    lists = jnp.concatenate(
-        [local_index.reshape(-1), halo_index.reshape(-1), block_count.reshape(-1)]
-    ).astype(F32)
-    lists = jnp.pad(lists, (0, D - lists.shape[0]))[None]
-    meta = jnp.concatenate([targets, lists, gains, jnp.zeros((5, D), F32)], axis=0)
+    hbm_spec = pl.BlockSpec(memory_space=pltpu.HBM)
     any_spec = pl.BlockSpec(memory_space=pl.ANY)
     vmem_spec = pl.BlockSpec(memory_space=pltpu.VMEM)
     dma = pltpu.SemaphoreType.DMA
@@ -558,7 +665,7 @@
             jax.ShapeDtypeStruct((D, D), F32),
             jax.ShapeDtypeStruct((1, D), F32),
         ),
-        in_specs=[any_spec] * 6,
+        in_specs=[hbm_spec] * 11,
         out_specs=(any_spec, any_spec, any_spec, vmem_spec),
         scratch_shapes=[
             pltpu.VMEM((LAYERS + 1, ROWS, D), BF),
@@ -566,16 +673,24 @@
             pltpu.VMEM((LAYERS, D, D), BF),
             pltpu.VMEM((4 * BLK, BLK), BF),
             pltpu.VMEM((2 * BLK, BLK), BF),
+            pltpu.VMEM((2, OWNERS), jnp.int32),
+            pltpu.VMEM((1, OWNERS), jnp.int32),
+            pltpu.VMEM((2, 4), jnp.int32),
+            pltpu.VMEM((2, 2), jnp.int32),
+            pltpu.VMEM((1, 2), jnp.int32),
+            pltpu.VMEM((1, D), F32),
+            pltpu.VMEM((8, D), F32),
             pltpu.VMEM((8, D), F32),
             pltpu.VMEM((LAYERS, 8, D), F32),
             pltpu.VMEM((2 * OWNERS, ROWS), BF),
+            pltpu.VMEM((ROWS, 2 * OWNERS), BF),
             pltpu.VMEM((ROWS, 2 * OWNERS), BF),
             pltpu.VMEM((ROWS, ROWS), BF),
             pltpu.VMEM((ROWS, ROWS), BF),
             pltpu.VMEM((ROWS, 2 * OWNERS), BF),
             pltpu.VMEM((2 * OWNERS, ROWS), BF),
-            pltpu.VMEM((2 * LAYERS, OWNERS, 2, D), BF),
-            pltpu.VMEM((2 * LAYERS, OWNERS, 2, D), BF),
+            pltpu.VMEM((2 * LAYERS + 1, OWNERS, 2, D), BF),
+            pltpu.VMEM((2 * LAYERS + 1, OWNERS, 2, D), BF),
             pltpu.VMEM((LAYERS, ROWS, D), F32),
             pltpu.VMEM((LAYERS, ROWS, D), F32),
             pltpu.VMEM((LAYERS, ROWS, BLK), F32),
@@ -587,18 +702,19 @@
             pltpu.VMEM((LAYERS, 4, 16, BLK), F32),
             pltpu.VMEM((LAYERS, 16, BLK), F32),
             pltpu.VMEM((LAYERS, 1, D), F32),
-            pltpu.VMEM((32, 1, D), F32),
-            pltpu.VMEM((1, D), F32),
-            pltpu.VMEM((4, 1, D), F32),
+            pltpu.VMEM((OWNERS, 1, D), F32),
+            pltpu.VMEM((ROWS, D), F32),
+            pltpu.VMEM((ROWS, D), F32),
             pltpu.VMEM((8, 16, BLK), F32),
+            dma((6,)),
             dma((5,)),
             dma((5,)),
             dma,
             dma((LAYERS,)),
             dma,
             dma,
-            dma((2 * LAYERS,)),
-            dma((2 * LAYERS,)),
+            dma((2 * LAYERS + 1,)),
+            dma((2 * LAYERS + 1,)),
             dma((LAYERS,)),
             dma((LAYERS,)),
             dma((LAYERS,)),
@@ -613,7 +729,7 @@
             dma((2,)),
         ],
         compiler_params=pltpu.CompilerParams(
-            collective_id=0, has_side_effects=True, vmem_limit_bytes=48 * 1024 * 1024
+            collective_id=0, has_side_effects=True, vmem_limit_bytes=64 * 1024 * 1024
         ),
     )(
         feats[0],
@@ -621,8 +737,22 @@
         local_vals.reshape(4 * BLK, BLK),
         halo_vals.reshape(2 * BLK, BLK),
         cotangent[0],
-        meta,
+        send_rows[0, 0].T,
+        send_count[0],
+        local_index[0, 0].T,
+        halo_index[0, 0],
+        block_count[0],
+        gains,
     )
+    results = (out_x, out_g, out_w, out_gg)
+    out_x, out_g, out_w, out_gg = pl.pallas_call(
+        settle,
+        out_shape=tuple(jax.ShapeDtypeStruct(a.shape, a.dtype) for a in results),
+        in_specs=[hbm_spec] * 4,
+        out_specs=(hbm_spec,) * 4,
+        scratch_shapes=[pltpu.VMEM(a.shape, a.dtype) for a in results] + [dma((4,)), dma((4,))],
+        compiler_params=pltpu.CompilerParams(vmem_limit_bytes=64 * 1024 * 1024),
+    )(*results)
     return out_x[None, None], out_g[None, None], out_w[None], out_gg
 
 

time: 115 us -> 103 us (0.90)
  local copies, waits for them, and re-layouts: 8.79 us -> 0 us
  Pallas kernels: 104 us -> 102 us
  other arithmetic: 1.55 us -> 0 us
    unnamed x18 -> x0, local copies, waits for them, and re-layouts: 7.54 us -> none
    pallas_call x1, Pallas kernels: 104 us -> 100 us  [on_device(): pl.pallas_call(kernel, out_shape=(jax.ShapeDtypeStruct((ROWS, D), BF), ja...]
    pallas_call x0 -> x1, Pallas kernels: none -> 1.86 us  [on_device(): pl.pallas_call(settle, out_shape=tuple((jax.ShapeDtypeStruct(a.shape, a.d...]
where the time goes in v2:
time: 103 us
  Pallas kernels  102 us (99%)
    pallas_call x1, Pallas kernels, on_device(): pl.pallas_call(kernel, out_shape=(jax.ShapeDtypeStruct((ROWS, D), BF), ja...  100 us

profile of v2, /device:TPU:1, one launch (start us, length us, event | category | flops | bytes accessed | tf_op | source)
XLA Modules:
  0.0 102.9 jit_solution(8484677747024453287)
XLA Ops:
  0.6 100.2 %shard_map.138 = (bf16[256,256]{1,0:T(8,128)(2,1)}, bf16[256,256]{1,0:T(8,128)(2,1)}, f32[256,256]{1,0:T(8,128)}, f32[1,256]{1,0:T(1,128)}) custom-call(bf16[256,256]{1,0:T(8,128)(2,1)} %bitcast.17, bf16[256,256]{1,0:T(8,128)(2,1)} %bitcast.18, bf16[512,128]{1,0:T(8,128)(2,1)} %bitcast.19, bf16[256,128]{1,0:T(8,128)(2,1)} %bitcast.21, ...), custom_call_target="tpu_custom_call" | custom-call | tf_op jit(solution)/shard_map/pallas_call | solution.py:660
  100.9 1.9 %shard_map.139 = (bf16[256,256]{1,0:T(8,128)(2,1)}, bf16[256,256]{1,0:T(8,128)(2,1)}, f32[256,256]{1,0:T(8,128)}, f32[1,256]{1,0:T(1,128)}) custom-call(bf16[256,256]{1,0:T(8,128)(2,1)} %get-tuple-element.12.refs_0_, bf16[256,256]{1,0:T(8,128)(2,1)} %get-tuple-element.13.refs_1_, f32[256,256]{1,0:T(8,128)} %get-tuple-element.14.refs_2_, ...), custom_call_target="tpu_custom_call" | custom-call | tf_op jit(solution)/shard_map/pallas_call | solution.py:748

commit v3 on v2

--- a/solution.py
+++ b/solution.py
@@ -96,6 +96,8 @@
     wc_out,
     gg_out,
     gg_in,
+    ggz_out,
+    ggz_in,
     base_out,
     base_in,
     filler,
@@ -116,6 +118,8 @@
     sem_c,
     sem_gg_send,
     sem_gg,
+    sem_ggz_send,
+    sem_ggz,
     sem_base_send,
     sem_base,
     sem_o_send,
@@ -176,6 +180,22 @@
         for dy in range(4)
         for dc in range(2)
     }
+    seat_of = [
+        [32 * seg_of[dx] + 8 * seat(seg_of[dx], z_by_distance[i]) for i in range(4)]
+        for dx in range(4)
+    ]
+    everywhere = sorted(
+        (
+            (dx, i, dy, dc)
+            for dx in range(4)
+            for i in range(4)
+            for dy in range(4)
+            for dc in range(2)
+        ),
+        key=lambda t: -(
+            (0, 1, 2, 1)[t[0]] + (2.5, 1.5, 1.0, 0.0)[t[1]] + (0, 1, 2, 1)[t[2]] + 0.1 * t[3]
+        ),
+    )
     in_order = sorted(
         ((i, dy, dc) for i in range(4) for dy in range(4) for dc in range(2)),
         key=lambda t: -((2.5, 1.5, 1.0, 0.0)[t[0]] + (0, 1, 2, 1)[t[1]] + 0.1 * t[2]),
@@ -190,15 +210,14 @@
                 barrier, inc=1, device_id=(xx, (4 * x + zo) * 8 + wv), device_id_type=MESH
             )
 
-    for dx in (2, 1, 3, 0):
-        for i, dy, dc in in_order:
-            if (dx, i, dy, dc) != (0, 3, 0, 0):
-                pl.semaphore_signal(
-                    barrier,
-                    inc=1,
-                    device_id=(seg_of[dx], base_of[i] + lane_of[dy, dc]),
-                    device_id_type=MESH,
-                )
+    for dx, i, dy, dc in everywhere:
+        if (dx, i, dy, dc) != (0, 3, 0, 0):
+            pl.semaphore_signal(
+                barrier,
+                inc=1,
+                device_id=(seg_of[dx], base_of[i] + lane_of[dy, dc]),
+                device_id_type=MESH,
+            )
 
     for copy in small:
         copy.wait()
@@ -279,20 +298,19 @@
                 pltpu.make_async_copy(weight, ws.at[l], sem_w.at[l]).start()
 
     def send_all(r, matrix, source):
-        for dx in (2, 1, 3, 0):
-            xx = seg_of[dx]
-            rows = mm(matrix[pl.ds(pl.multiple_of(64 * xx, 64), 64), :], source)
-            sent[r, pl.ds(32 * xx, 32)] = rows.astype(BF).reshape(32, 2, D)
-
-            for i, dy, dc in in_order:
-                cell = base_of[i] + lane_of[dy, dc]
-                v = 32 * xx + 8 * seat(xx, z_by_distance[i]) + lane_of[dy, dc]
-                if (dx, i, dy, dc) == (0, 3, 0, 0):
-                    pltpu.make_async_copy(sent.at[r, v], got.at[r, v], sem_got.at[r]).start()
-                else:
-                    remote(
-                        sent.at[r, v], got.at[r, me], sem_send.at[r], sem_got.at[r], (xx, cell)
-                    ).start()
+        sent[r] = mm(matrix[...], source).astype(BF).reshape(OWNERS, 2, D)
+        for dx, i, dy, dc in everywhere:
+            v = seat_of[dx][i] + lane_of[dy, dc]
+            if (dx, i, dy, dc) == (0, 3, 0, 0):
+                pltpu.make_async_copy(sent.at[r, v], got.at[r, v], sem_got.at[r]).start()
+            else:
+                remote(
+                    sent.at[r, v],
+                    got.at[r, me],
+                    sem_send.at[r],
+                    sem_got.at[r],
+                    (seg_of[dx], base_of[i] + lane_of[dy, dc]),
+                ).start()
 
     def receive(r):
         wait_for(got.at[r], sem_got.at[r])
@@ -474,8 +492,10 @@
                 remote(wc_out.at[l], place, sem_c_send.at[l], sem_c, dev(l, zl, ww)).start()
 
     def gains_out(l):
-        place = gg_in.at[(4 * x + zl) * 8 + wv]
+        place = gg_in.at[8 * x + wv] if l > 0 else gg_in.at[(4 * x + zl) * 8 + wv]
         for i, dy, dc in in_order:
+            if l > 0 and i < 3:
+                continue
             cell = base_of[i] + lane_of[dy, dc]
             if (i, dy, dc) == (3, 0, 0):
 
@@ -558,10 +578,11 @@
             tiles_z(l + 1)
         if l in (0, 1):
             tiles_home(l + 2)
+        if l == 0:
+            tiles_home(0)
         if l > 0:
             gs[l] = (gs[l + 1].astype(F32) + own + mm(pick_t[...], receive(r))).astype(BF)
 
-    tiles_home(0)
     tiles_home(1)
 
     @pl.when(x == 0)
@@ -574,8 +595,22 @@
         gs[0] = (base_in[...] + spread).astype(BF)
         pltpu.make_async_copy(gs.at[0], out_g, sem_o.at[1]).start()
 
-    wait_for(gg_in, sem_gg)
-    out_gg[...] = jnp.sum(gg_in[...], axis=0) * SCALE
+    @pl.when(x == 0)
+    def _():
+        wait_for(gg_in, sem_gg)
+        out_gg[...] = jnp.sum(gg_in[...], axis=0) * SCALE
+
+    @pl.when(x != 0)
+    def _():
+        wait_for(gg_in.at[pl.ds(0, 32)], sem_gg)
+        ggz_out[...] = jnp.sum(gg_in[0:32], axis=0)
+        for i in range(3):
+            remote(ggz_out, ggz_in.at[zl], sem_ggz_send, sem_ggz, (x, base_of[i] + wv)).start()
+        pltpu.make_async_copy(ggz_out, ggz_in.at[zl], sem_ggz).start()
+        wait_for(ggz_in, sem_ggz)
+        out_gg[...] = jnp.sum(ggz_in[...], axis=0) * SCALE
+        wait_for(ggz_in.at[pl.ds(0, 3)], sem_ggz_send)
+
 
     wait_for(out_x, sem_o.at[0])
     wait_for(out_g, sem_o.at[1])
@@ -614,12 +649,12 @@
         @pl.when(x == l)
         def _():
             wait_for(filler.at[pl.ds(0, 7)], sem_c_send.at[l])
-            wait_for(gg_in.at[pl.ds(0, 31)], sem_gg_send.at[l])
+            wait_for(gg_in.at[pl.ds(0, 7 if l else 31)], sem_gg_send.at[l])
 
         @pl.when(x != l)
         def _():
             wait_for(filler, sem_c_send.at[l])
-            wait_for(gg_in.at[pl.ds(0, 32)], sem_gg_send.at[l])
+            wait_for(gg_in.at[pl.ds(0, 8 if l else 32)], sem_gg_send.at[l])
 
         @pl.when(jnp.logical_and(diag, x != l))
         def _():
@@ -703,6 +738,8 @@
             pltpu.VMEM((LAYERS, 16, BLK), F32),
             pltpu.VMEM((LAYERS, 1, D), F32),
             pltpu.VMEM((OWNERS, 1, D), F32),
+            pltpu.VMEM((1, D), F32),
+            pltpu.VMEM((4, 1, D), F32),
             pltpu.VMEM((ROWS, D), F32),
             pltpu.VMEM((ROWS, D), F32),
             pltpu.VMEM((8, 16, BLK), F32),
@@ -722,6 +759,8 @@
             dma((LAYERS,)),
             dma,
             dma((LAYERS,)),
+            dma,
+            dma,
             dma,
             dma,
             dma,

time: 103 us -> 101 us (0.981)
  Pallas kernels: 102 us -> 100 us
    pallas_call x1, Pallas kernels: 100 us -> 98.4 us  [on_device(): pl.pallas_call(kernel, out_shape=(jax.ShapeDtypeStruct((ROWS, D), BF), ja...]
where the time goes in v3:
time: 101 us
  Pallas kernels  100 us (99%)
    pallas_call x1, Pallas kernels, on_device(): pl.pallas_call(kernel, out_shape=(jax.ShapeDtypeStruct((ROWS, D), BF), ja...  98.4 us

profile of v3, /device:TPU:1, one launch (start us, length us, event | category | flops | bytes accessed | tf_op | source)
XLA Modules:
  0.0 101.0 jit_solution(12071755506885174779)
XLA Ops:
  0.6 98.4 %shard_map.138 = (bf16[256,256]{1,0:T(8,128)(2,1)}, bf16[256,256]{1,0:T(8,128)(2,1)}, f32[256,256]{1,0:T(8,128)}, f32[1,256]{1,0:T(1,128)}) custom-call(bf16[256,256]{1,0:T(8,128)(2,1)} %bitcast.17, bf16[256,256]{1,0:T(8,128)(2,1)} %bitcast.18, bf16[512,128]{1,0:T(8,128)(2,1)} %bitcast.19, bf16[256,128]{1,0:T(8,128)(2,1)} %bitcast.21, ...), custom_call_target="tpu_custom_call" | custom-call | tf_op jit(solution)/shard_map/pallas_call | solution.py:695
  99.0 1.9 %shard_map.139 = (bf16[256,256]{1,0:T(8,128)(2,1)}, bf16[256,256]{1,0:T(8,128)(2,1)}, f32[256,256]{1,0:T(8,128)}, f32[1,256]{1,0:T(1,128)}) custom-call(bf16[256,256]{1,0:T(8,128)(2,1)} %get-tuple-element.12.refs_0_, bf16[256,256]{1,0:T(8,128)(2,1)} %get-tuple-element.13.refs_1_, f32[256,256]{1,0:T(8,128)} %get-tuple-element.14.refs_2_, ...), custom_call_target="tpu_custom_call" | custom-call | tf_op jit(solution)/shard_map/pallas_call | solution.py:787
